TPU v7x, 32 devices: a whole 2x2x4 slice. The times are simulated.
32 devices in a mesh: section: 16 (over z, y, x), tp: 2 (over core).
Axes of the slice: x: 2, y: 2, z: 4, core: 2. Of those that a mesh axis runs over, the one named last changes fastest.
Arguments:
- queries: bfloat16 [6144, 3072], P('section', 'tp'), may hold values from -60 to 60
- keys: bfloat16 [6144, 3072], P('section', 'tp'), may hold values from -6 to 6
- values: bfloat16 [6144, 3072], P('section', 'tp'), may hold values from -40 to 40
- cotangent: bfloat16 [6144, 3072], P('section', 'tp'), may hold values from -6 to 6
- doc_ids: int32 [6144], P('section'), may hold values from 0 to 3, never falling along the last dimension, each value on 1 to 3072 neighbouring positions
- gain: float32 [3072], P('tp'), may hold values from 0.1 to 1.9
Outputs:
- normed: bfloat16 [6144, 3072], P('section', 'tp')
- grad_queries: bfloat16 [6144, 3072], P('section', 'tp')
- grad_keys: bfloat16 [6144, 3072], P('section', 'tp')
- grad_values: bfloat16 [6144, 3072], P('section', 'tp')
All inputs are finite; a program needn't handle non-finite values.
Results may differ from a plain program's by a relative error of at most 0.009.
Values may be sent and summed in bfloat16 or wider, within the bound.
A program may use at most 192 MiB of HBM per device.

v0:
```python
import jax
import jax.numpy as jnp
from jax import lax
from jax.sharding import PartitionSpec as P

HS = 128
BAND_DEV = 2


def from_behind(value, axis, steps):
    count = lax.axis_size(axis)
    initial, last = (max(0, -steps), min(count, count - steps))
    return lax.ppermute(value, axis, [(source, source + steps) for source in range(initial, last)])


def band_mask(query_pos, query_doc, key_pos, key_doc, window):
    distance = query_pos[:, None] - key_pos[None, :]
    return (
        (distance >= 0)
        & (distance < window)
        & (key_pos[None, :] >= 0)
        & (query_doc[:, None] == key_doc[None, :])
    )


def body(queries, keys, values, cotangent, doc_ids, gain):
    tok_rows = queries.shape[0]
    head_count = queries.shape[1] // HS
    feature_total = queries.shape[1] * lax.axis_size("tp")
    section_index = lax.axis_index("section")
    window = BAND_DEV * tok_rows
    score_scale = HS ** (-0.5)
    offsets = jnp.arange(tok_rows, dtype=jnp.int32)
    own_pos = section_index * tok_rows + offsets
    query_heads = queries.reshape(tok_rows, head_count, HS)
    blocks = [(keys, values, doc_ids)]
    current = (keys, values, doc_ids)
    for distance in range(1, BAND_DEV + 1):
        current = from_behind((current[0], current[1], current[2]), "section", 1)
        blocks.append(current)
    key_band = jnp.concatenate([entry[0] for entry in blocks], 0).reshape(-1, head_count, HS)
    value_band = jnp.concatenate([entry[1] for entry in blocks], 0).reshape(-1, head_count, HS)
    doc_band = jnp.concatenate([entry[2] for entry in blocks], 0)
    key_pos = jnp.concatenate(
        [(section_index - distance) * tok_rows + offsets for distance in range(BAND_DEV + 1)], 0
    )
    visible = band_mask(own_pos, doc_ids, key_pos, doc_band, window)
    scores = (
        jnp.einsum("qhd,khd->hqk", query_heads, key_band, preferred_element_type=jnp.float32)
        * score_scale
    )
    scores = jnp.where(visible[None], scores, -1e30)
    row_max = jnp.max(scores, axis=-1, keepdims=True)
    log_total = row_max + jnp.log(jnp.sum(jnp.exp(scores - row_max), axis=-1, keepdims=True))
    weights = jnp.exp(scores - log_total)
    weights_b = weights.astype(jnp.bfloat16)
    attended = jnp.einsum(
        "hqk,khd->qhd", weights_b, value_band, preferred_element_type=jnp.float32
    ).reshape(tok_rows, -1)
    squares = lax.psum(jnp.sum(attended * attended, axis=-1), "tp")
    inverse = lax.rsqrt(squares / feature_total + 1e-05)[:, None]
    normed = (attended * inverse * gain).astype(jnp.bfloat16)
    scaled_grad = cotangent.astype(jnp.float32) * gain
    inner_sum = lax.psum(jnp.sum(scaled_grad * attended, axis=-1), "tp")[:, None]
    grad_out = (inverse * scaled_grad - attended * inverse**3 * inner_sum / feature_total).astype(
        jnp.bfloat16
    )
    grad_heads = grad_out.reshape(tok_rows, head_count, HS)
    row_delta = jnp.sum(
        grad_heads.astype(jnp.float32) * attended.reshape(tok_rows, head_count, HS), axis=-1
    ).T
    grad_weights = jnp.einsum(
        "qhd,khd->hqk", grad_heads, value_band, preferred_element_type=jnp.float32
    )
    dscore = (weights * (grad_weights - row_delta[:, :, None])).astype(jnp.bfloat16)
    grad_query = (
        jnp.einsum("hqk,khd->qhd", dscore, key_band, preferred_element_type=jnp.float32)
        * score_scale
    )
    key_terms = (
        jnp.einsum("hqk,qhd->khd", dscore, query_heads, preferred_element_type=jnp.float32)
        * score_scale
    ).reshape(-1, queries.shape[1])
    value_terms = jnp.einsum(
        "hqk,qhd->khd", weights_b, grad_heads, preferred_element_type=jnp.float32
    ).reshape(-1, queries.shape[1])
    grad_key = key_terms[:tok_rows]
    grad_value = value_terms[:tok_rows]
    for distance in range(1, BAND_DEV + 1):
        partial_value = (
            key_terms[distance * tok_rows : (distance + 1) * tok_rows],
            value_terms[distance * tok_rows : (distance + 1) * tok_rows],
        )
        arrived = from_behind((partial_value[0], partial_value[1]), "section", -distance)
        grad_key = grad_key + arrived[0]
        grad_value = grad_value + arrived[1]
    return (
        normed,
        grad_query.reshape(tok_rows, -1).astype(jnp.bfloat16),
        grad_key.astype(jnp.bfloat16),
        grad_value.astype(jnp.bfloat16),
    )


def solution(mesh):
    return jax.shard_map(
        body,
        mesh=mesh,
        in_specs=(
            P("section", "tp"),
            P("section", "tp"),
            P("section", "tp"),
            P("section", "tp"),
            P("section"),
            P("tp"),
        ),
        out_specs=(P("section", "tp"), P("section", "tp"), P("section", "tp"), P("section", "tp")),
        check_vma=False,
    )
```

profile of v0, /device:TPU:14, one launch (start us, length us, event | category | flops | bytes accessed | tf_op | source)
XLA Modules:
  0.0 454.5 jit_solution(10383592856300185346)
XLA Ops:
  0.6 0.0 copy-start.11
  0.6 0.0 copy-start.7
  0.7 3.5 collective-permute-start
  4.2 1.7 copy.34
  5.9 0.0 copy-start.4
  5.9 3.4 collective-permute-start.4
  9.3 22.4 %collective-permute-done = bf16[384,1536]{1,0:T(8,128)(2,1)S(1)} collective-permute-done((bf16[384,1536]{1,0:T(8,128)(2,1)}, bf16[384,1536]{1,0:T(8,128)(2,1)S(1)}, u32[]{:S(2)}, u32[]{:S(2)}) %collective-permute-start) | collective-permute-done | bytes 1179680 | tf_op jit(solution)/shard_map/ppermute | solution.py:13
  31.7 5.2 %collective-permute-start.1 = (bf16[384,1536]{1,0:T(8,128)(2,1)S(1)}, bf16[384,1536]{1,0:T(8,128)(2,1)}, u32[]{:S(2)}, u32[]{:S(2)}) collective-permute-start(bf16[384,1536]{1,0:T(8,128)(2,1)S(1)} %collective-permute-done), channel_id=1, source_target_pairs={{0,2},{2,4},{4,6},{6,8},{8,10},{10,12},{12,14},{14,16},{16,18},{18... | collective-permute-start | bytes 3538952 | tf_op jit(solution)/shard_map/ppermute | solution.py:13
  36.9 0.0 copy-done.11
  37.0 1.9 collective-permute-start.2
  38.9 42.4 %collective-permute-done.2 = s32[384]{0:T(512)} collective-permute-done((s32[384]{0:T(512)S(1)}, s32[384]{0:T(512)}, u32[]{:S(2)}, u32[]{:S(2)}) %collective-permute-start.2) | collective-permute-done | bytes 1568 | tf_op jit(solution)/shard_map/ppermute | solution.py:13
  81.3 5.2 %collective-permute-start.3 = (s32[384]{0:T(512)}, s32[384]{0:T(512)}, u32[]{:S(2)}, u32[]{:S(2)}) collective-permute-start(s32[384]{0:T(512)} %collective-permute-done.2), channel_id=1, source_target_pairs={{0,2},{2,4},{4,6},{6,8},{8,10},{10,12},{12,14},{14,16},{16,18},{18... | collective-permute-start | bytes 4616 | tf_op jit(solution)/shard_map/ppermute | solution.py:13
  86.5 0.6 broadcast_compare_fusion
  87.1 0.0 copy-done.7
  87.1 1.4 copy.35
  88.5 0.0 collective-permute-done.4
  88.5 1.9 collective-permute-start.5
  90.4 0.0 collective-permute-done.3
  90.4 0.7 pad_add_fusion.1
  91.1 2.9 fusion.8
  94.0 0.0 copy-done.4
  94.0 0.0 copy-done.6
  94.0 0.0 collective-permute-done.1
  94.0 2.1 pad_maximum_fusion
  96.1 3.9 copy.32
  100.0 17.3 %collective-permute-done.5 = bf16[384,1536]{0,1:T(8,128)(2,1)} collective-permute-done((bf16[384,1536]{0,1:T(8,128)(2,1)}, bf16[384,1536]{0,1:T(8,128)(2,1)}, u32[]{:S(2)}, u32[]{:S(2)}) %collective-permute-start.5) | collective-permute-done | bytes 1179680 | tf_op jit(solution)/shard_map/ppermute | solution.py:13
  117.3 2.1 pad_maximum_fusion.1
  119.4 0.0 copy-done.2
  119.4 0.0 copy-done.5
  119.4 9.2 %fusion.11 = (f32[12,384]{1,0:T(8,128)S(1)}, f32[12,384,1152]{1,2,0:T(8,128)}) fusion(bf16[1152,12,128]{0,2,1:T(8,128)(2,1)S(1)} %bitcast.39, bf16[384,12,128]{0,2,1:T(8,128)(2,1)S(1)} %bitcast.48, pred[384,1152]{0,1:T(8,128)(4,1)S(1)} %copy-done.5), kind=kOutput, calls=%fused_computation.37 | convolution fusion | flops 1374875136 | bytes 26413056 | tf_op jit(solution)/shard_map/qhd,khd->hqk/dot_general | solution.py:49
  128.6 9.0 %exponential_reduce_fusion = f32[12,384]{1,0:T(8,128)S(1)} fusion(f32[12,384,1152]{1,2,0:T(8,128)} %get-tuple-element.25, f32[12,384]{1,0:T(8,128)S(1)} %get-tuple-element.24), kind=kLoop, calls=%fused_computation.3 | loop fusion | flops 10612224 | bytes 21270528 | tf_op jit(solution)/shard_map/reduce_sum | solution.py:54
  137.6 0.0 copy-start.8
  137.6 0.0 copy-done
  137.6 11.9 %fusion.5 = (f32[384]{0:T(512)S(1)}, f32[12,128,384]{2,1,0:T(8,128)}) fusion(bf16[1152,12,128]{0,2,1:T(8,128)(2,1)S(1)} %bitcast.42, f32[12,384,1152]{1,2,0:T(8,128)} %get-tuple-element.25, f32[12,384]{1,0:T(8,128)S(1)} %log_add_fusion), kind=kOutput, calls=%fused_computation.15 | convolution fusion | flops 1370750592 | bytes 27151872 | tf_op jit(solution)/shard_map/hqk,khd->qhd/dot_general | solution.py:57
  149.5 3.1 copy.39
  152.6 2.4 multiply_reduce_fusion
  155.0 3.2 all-reduce
  158.2 0.7 multiply_multiply_fusion
  158.9 4.4 subtract_convert_fusion
  163.3 2.4 copy.42
  165.6 2.4 fusion.4
  168.0 16.1 %multiply_convert_fusion = bf16[12,384,1152]{1,2,0:T(8,128)(2,1)} fusion(bf16[384,12,128]{0,2,1:T(8,128)(2,1)S(1)} %bitcast.46, bf16[1152,12,128]{0,2,1:T(8,128)(2,1)} %bitcast.41, f32[12,384,1152]{1,2,0:T(8,128)} %get-tuple-element.25, f32[12,384]{1,0:T(8,128)S(1)} %bitcast.56, f32[12,384]{1,0:T(8,128)S(1)} %copy-done.9), kind=kOutput, calls=%fused_computation.1 | convolution fusion | flops 1380188160 | bytes 36605952 | tf_op jit(solution)/shard_map/qhd,khd->hqk/dot_general | solution.py:72
  184.2 10.8 %multiply_bitcast_fusion = f32[1152,12,128]{0,2,1:T(8,128)} fusion(bf16[12,384,1152]{1,2,0:T(8,128)(2,1)} %multiply_convert_fusion, bf16[384,12,128]{0,2,1:T(8,128)(2,1)} %bitcast.47), kind=kOutput, calls=%fused_computation.5 | convolution fusion | flops 1360723968 | bytes 18874368 | tf_op jit(solution)/shard_map/hqk,qhd->khd/dot_general | solution.py:81
  194.9 6.2 %fusion.10 = (f32[384,12,128]{0,2,1:T(8,128)}, f32[384,12,128]{0,2,1:T(8,128)}, f32[384,12,128]{0,2,1:T(8,128)}) fusion(f32[1152,12,128]{0,2,1:T(8,128)} %multiply_bitcast_fusion), kind=kLoop, calls=%fused_computation.36 | loop fusion | bytes 14155776 | tf_op jit(solution)/shard_map/slice | solution.py:91
  201.1 3.1 copy.50
  204.2 1.9 collective-permute-start.7
  206.1 3.1 copy.48
  209.2 3.5 collective-permute-start.6
  212.7 13.9 %convolution_bitcast_fusion = f32[1152,12,128]{0,2,1:T(8,128)} fusion(bf16[384,12,128]{0,2,1:T(8,128)(2,1)} %bitcast.45, f32[12,384,1152]{1,2,0:T(8,128)} %get-tuple-element.25, f32[12,384]{1,0:T(8,128)} %copy-done.8), kind=kOutput, calls=%fused_computation.6 | convolution fusion | flops 1369571328 | bytes 29509632 | tf_op jit(solution)/shard_map/hqk,qhd->khd/dot_general | solution.py:84
  226.6 6.1 %fusion.9 = (f32[384,12,128]{0,2,1:T(8,128)}, f32[384,12,128]{0,2,1:T(8,128)}, f32[384,12,128]{0,2,1:T(8,128)}) fusion(f32[1152,12,128]{0,2,1:T(8,128)} %convolution_bitcast_fusion), kind=kLoop, calls=%fused_computation.35 | loop fusion | bytes 14155776 | tf_op jit(solution)/shard_map/slice | solution.py:92
  232.7 3.1 copy.54
  235.8 2.3 collective-permute-start.9
  238.0 3.1 copy.52
  241.1 3.5 collective-permute-start.8
  244.6 7.2 %multiply_convert_fusion.1 = bf16[12,128,384]{2,1,0:T(8,128)(2,1)} fusion(bf16[1152,12,128]{0,2,1:T(8,128)(2,1)S(1)} %bitcast.40, bf16[12,384,1152]{1,2,0:T(8,128)(2,1)} %multiply_convert_fusion), kind=kOutput, calls=%fused_computation.18 | convolution fusion | flops 1360134144 | bytes 15335424 | tf_op jit(solution)/shard_map/hqk,khd->qhd/dot_general | solution.py:77
  251.9 2.5 copy.55
  254.4 1.9 copy.49
  256.3 2.0 copy.53
  258.4 100.7 %collective-permute-done.7 = f32[384,1536]{1,0:T(8,128)} collective-permute-done((f32[384,1536]{1,0:T(8,128)}, f32[384,1536]{1,0:T(8,128)}, u32[]{:S(2)}, u32[]{:S(2)}) %collective-permute-start.7) | collective-permute-done | bytes 2359328 | tf_op jit(solution)/shard_map/ppermute | solution.py:13
  359.1 0.0 collective-permute-done.6
  359.1 4.7 %add_convert_fusion.1 = bf16[384,1536]{1,0:T(8,128)(2,1)} fusion(f32[384,1536]{1,0:T(8,128)} %collective-permute-done.7, f32[384,1536]{1,0:T(8,128)} %copy.49, f32[384,1536]{1,0:T(8,128)} %collective-permute-done.6), kind=kLoop, calls=%fused_computation.17 | loop fusion | flops 1769472 | bytes 8257536 | tf_op jit(solution)/shard_map/convert_element_type | solution.py:100
  363.7 45.4 %collective-permute-done.9 = f32[384,1536]{1,0:T(8,128)} collective-permute-done((f32[384,1536]{1,0:T(8,128)}, f32[384,1536]{1,0:T(8,128)}, u32[]{:S(2)}, u32[]{:S(2)}) %collective-permute-start.9) | collective-permute-done | bytes 2359328 | tf_op jit(solution)/shard_map/ppermute | solution.py:13
  409.2 41.4 %collective-permute-done.8 = f32[384,1536]{1,0:T(8,128)} collective-permute-done((f32[384,1536]{1,0:T(8,128)}, f32[384,1536]{1,0:T(8,128)}, u32[]{:S(2)}, u32[]{:S(2)}) %collective-permute-start.8) | collective-permute-done | bytes 2359328 | tf_op jit(solution)/shard_map/ppermute | solution.py:13
  450.5 3.9 add_convert_fusion
  (17 shorter events, 0.1 us)
Async XLA Ops:
  0.6 36.3 %copy-start.11 = (s32[384]{0:T(512)S(1)}, s32[384]{0:T(512)}, u32[]{:S(2)}) copy-start(s32[384]{0:T(512)} %param.10) | copy-start | bytes 4612
  0.6 86.5 %copy-start.7 = (bf16[384,1536]{1,0:T(8,128)(2,1)S(1)}, bf16[384,1536]{1,0:T(8,128)(2,1)}, u32[]{:S(2)}) copy-start(bf16[384,1536]{1,0:T(8,128)(2,1)} %param.6) | copy-start | bytes 3538948
  0.7 31.1 %collective-permute-start = (bf16[384,1536]{1,0:T(8,128)(2,1)}, bf16[384,1536]{1,0:T(8,128)(2,1)S(1)}, u32[]{:S(2)}, u32[]{:S(2)}) collective-permute-start(bf16[384,1536]{1,0:T(8,128)(2,1)} %param.8), channel_id=1, source_target_pairs={{0,2},{2,4},{4,6},{6,8},{8,10},{10,12},{12,14},{14,16},{16,18},{18... | collective-permute-start | bytes 3538952 | tf_op jit(solution)/shard_map/ppermute | solution.py:13
  5.9 88.1 %copy-start.4 = (bf16[384,1536]{0,1:T(8,128)(2,1)}, bf16[384,1536]{0,1:T(8,128)(2,1)S(1)}, u32[]{:S(2)}) copy-start(bf16[384,1536]{0,1:T(8,128)(2,1)S(1)} %copy.34) | copy-start | bytes 3538948
  5.9 82.6 %collective-permute-start.4 = (bf16[384,1536]{0,1:T(8,128)(2,1)S(1)}, bf16[384,1536]{0,1:T(8,128)(2,1)}, u32[]{:S(2)}, u32[]{:S(2)}) collective-permute-start(bf16[384,1536]{0,1:T(8,128)(2,1)S(1)} %copy.34), channel_id=1, source_target_pairs={{0,2},{2,4},{4,6},{6,8},{8,10},{10,12},{12,14},{14,16},{16,18},{18... | collective-permute-start | bytes 3538952 | tf_op jit(solution)/shard_map/ppermute | solution.py:13
  31.7 62.3 %copy-start.6 = (bf16[384,1536]{1,0:T(8,128)(2,1)}, bf16[384,1536]{1,0:T(8,128)(2,1)S(1)}, u32[]{:S(2)}) copy-start(bf16[384,1536]{1,0:T(8,128)(2,1)S(1)} %collective-permute-done) | copy-start | bytes 3538948
  31.7 62.3 %collective-permute-start.1 = (bf16[384,1536]{1,0:T(8,128)(2,1)S(1)}, bf16[384,1536]{1,0:T(8,128)(2,1)}, u32[]{:S(2)}, u32[]{:S(2)}) collective-permute-start(bf16[384,1536]{1,0:T(8,128)(2,1)S(1)} %collective-permute-done), channel_id=1, source_target_pairs={{0,2},{2,4},{4,6},{6,8},{8,10},{10,12},{12,14},{14,16},{16,18},{18... | collective-permute-start | bytes 3538952 | tf_op jit(solution)/shard_map/ppermute | solution.py:13
  37.0 44.4 %collective-permute-start.2 = (s32[384]{0:T(512)S(1)}, s32[384]{0:T(512)}, u32[]{:S(2)}, u32[]{:S(2)}) collective-permute-start(s32[384]{0:T(512)S(1)} %copy-done.11), channel_id=1, source_target_pairs={{0,2},{2,4},{4,6},{6,8},{8,10},{10,12},{12,14},{14,16},{16,18},{18... | collective-permute-start | bytes 4616 | tf_op jit(solution)/shard_map/ppermute | solution.py:13
  81.3 9.1 %collective-permute-start.3 = (s32[384]{0:T(512)}, s32[384]{0:T(512)}, u32[]{:S(2)}, u32[]{:S(2)}) collective-permute-start(s32[384]{0:T(512)} %collective-permute-done.2), channel_id=1, source_target_pairs={{0,2},{2,4},{4,6},{6,8},{8,10},{10,12},{12,14},{14,16},{16,18},{18... | collective-permute-start | bytes 4616 | tf_op jit(solution)/shard_map/ppermute | solution.py:13
  88.5 28.8 %collective-permute-start.5 = (bf16[384,1536]{0,1:T(8,128)(2,1)}, bf16[384,1536]{0,1:T(8,128)(2,1)}, u32[]{:S(2)}, u32[]{:S(2)}) collective-permute-start(bf16[384,1536]{0,1:T(8,128)(2,1)} %collective-permute-done.4), channel_id=1, source_target_pairs={{0,2},{2,4},{4,6},{6,8},{8,10},{10,12},{12,14},{14,16},{16,18},{18... | collective-permute-start | bytes 3538952 | tf_op jit(solution)/shard_map/ppermute | solution.py:13
  100.0 19.4 %copy-start.2 = (bf16[384,1536]{0,1:T(8,128)(2,1)S(1)}, bf16[384,1536]{0,1:T(8,128)(2,1)}, u32[]{:S(2)}) copy-start(bf16[384,1536]{0,1:T(8,128)(2,1)} %copy.35) | copy-start | bytes 3538948
  100.0 19.4 %copy-start.5 = (pred[384,1152]{0,1:T(8,128)(4,1)S(1)}, pred[384,1152]{0,1:T(8,128)(4,1)}, u32[]{:S(2)}) copy-start(pred[384,1152]{0,1:T(8,128)(4,1)} %fusion.8) | copy-start | bytes 1327108
  128.6 9.0 %copy-start = (bf16[1152,1536]{0,1:T(8,128)(2,1)S(1)}, bf16[1152,1536]{0,1:T(8,128)(2,1)}, u32[]{:S(2)}) copy-start(bf16[1152,1536]{0,1:T(8,128)(2,1)} %copy.32) | copy-start | bytes 10616836
  137.6 11.9 %copy-start.8 = (f32[12,384]{1,0:T(8,128)}, f32[12,384]{1,0:T(8,128)S(1)}, u32[]{:S(2)}) copy-start(f32[12,384]{1,0:T(8,128)S(1)} %log_add_fusion) | copy-start | bytes 55300
  149.5 3.1 copy-start.10
  165.6 2.4 copy-start.1
  165.6 2.4 copy-start.9
  204.2 154.9 %collective-permute-start.7 = (f32[384,1536]{1,0:T(8,128)}, f32[384,1536]{1,0:T(8,128)}, u32[]{:S(2)}, u32[]{:S(2)}) collective-permute-start(f32[384,1536]{1,0:T(8,128)} %copy.50), channel_id=1, source_target_pairs={{4,0},{6,2},{8,4},{10,6},{12,8},{14,10},{16,12},{18,14},{20,16},{2... | collective-permute-start | bytes 7077896 | tf_op jit(solution)/shard_map/ppermute | solution.py:13
  209.2 149.9 %collective-permute-start.6 = (f32[384,1536]{1,0:T(8,128)}, f32[384,1536]{1,0:T(8,128)}, u32[]{:S(2)}, u32[]{:S(2)}) collective-permute-start(f32[384,1536]{1,0:T(8,128)} %copy.48), channel_id=1, source_target_pairs={{2,0},{4,2},{6,4},{8,6},{10,8},{12,10},{14,12},{16,14},{18,16},{20... | collective-permute-start | bytes 7077896 | tf_op jit(solution)/shard_map/ppermute | solution.py:13
  235.8 173.4 %collective-permute-start.9 = (f32[384,1536]{1,0:T(8,128)}, f32[384,1536]{1,0:T(8,128)}, u32[]{:S(2)}, u32[]{:S(2)}) collective-permute-start(f32[384,1536]{1,0:T(8,128)} %copy.54), channel_id=1, source_target_pairs={{4,0},{6,2},{8,4},{10,6},{12,8},{14,10},{16,12},{18,14},{20,16},{2... | collective-permute-start | bytes 7077896 | tf_op jit(solution)/shard_map/ppermute | solution.py:13
  241.1 209.4 %collective-permute-start.8 = (f32[384,1536]{1,0:T(8,128)}, f32[384,1536]{1,0:T(8,128)}, u32[]{:S(2)}, u32[]{:S(2)}) collective-permute-start(f32[384,1536]{1,0:T(8,128)} %copy.52), channel_id=1, source_target_pairs={{2,0},{4,2},{6,4},{8,6},{10,8},{12,10},{14,12},{16,14},{18,16},{20... | collective-permute-start | bytes 7077896 | tf_op jit(solution)/shard_map/ppermute | solution.py:13
  251.9 2.5 copy-start.3
where the time goes:
time: 455 us; the launch traced here: 454 us
  waiting for transfers between devices  270 us (59%)
  matrix products  69.1 us (15%)
  local copies, waits for them, and re-layouts  43.6 us (10%)
  other arithmetic  35.8 us (8%)
  starting transfers between devices  32.3 us (7%)
    ppermute x10, waiting for transfers between devices, from_behind(): lax.ppermute(value, axis, [(source, source + steps) for source in range(i...  270 us
    ppermute x10, starting transfers between devices, from_behind(): lax.ppermute(value, axis, [(source, source + steps) for source in range(i...  32.3 us
    dot_general x1, matrix products, body(): jnp.einsum('qhd,khd->hqk', grad_heads, value_band, preferred_element_type...  16.1 us
    dot_general x1, matrix products, body(): jnp.einsum('hqk,qhd->khd', weights_b, grad_heads, preferred_element_type=...  13.9 us
    slice x3, local copies, waits for them, and re-layouts, body(): key_terms[distance * tok_rows:(distance + 1) * tok_rows]  12.3 us
    slice x3, local copies, waits for them, and re-layouts, body(): value_terms[distance * tok_rows:(distance + 1) * tok_rows]  12.2 us
    dot_general x1, matrix products, body(): jnp.einsum('hqk,khd->qhd', weights_b, value_band, preferred_element_type=...  11.9 us
    dot_general x1, matrix products, body(): jnp.einsum('hqk,qhd->khd', dscore, query_heads, preferred_element_type=jn...  10.8 us
  transfers between devices with their start and end apart: 10, of which 6 were waited for; matrix products, arithmetic and copies ran while one was open for 13% of the time, Pallas kernels for 0%

commit v1 on v0

v1 whole, which is shorter than its diff:
```python
import functools
import math

import jax
import jax.numpy as jnp
from jax import lax
from jax.experimental import pallas as pl
from jax.experimental.pallas import tpu as pltpu
from jax.sharding import PartitionSpec as P

HS = 128
GROUPS = 4
MESH = pl.DeviceIdType.MESH
LOG2E = math.log2(math.e)
HIDDEN = -1e30
NT = (((1,), (1,)), ((), ()))


def nt_dot(a, b):
    return lax.dot_general(a, b, NT, preferred_element_type=jnp.float32)


def nn_dot(a, b):
    return jnp.dot(a, b, preferred_element_type=jnp.float32)


def kernel(
    n,
    tp,
    q_ref,
    k_ref,
    v_ref,
    cot_ref,
    doc_ref,
    gain_ref,
    normed_ref,
    dq_ref,
    dk_ref,
    dv_ref,
    kv_buf,
    qo_buf,
    do_ref,
    att_ref,
    w_ref,
    bias_ref,
    bias_t_ref,
    dk_acc,
    dv_acc,
    doc_own,
    doc_buf,
    sums,
    sums_buf,
    stat_col,
    stat_own,
    stat_buf,
    kv_send,
    kv_recv,
    qo_send,
    qo_recv,
    doc_send,
    doc_recv,
    sums_send,
    sums_recv,
    stat_send,
    stat_recv,
):
    rows, cols = q_ref.shape
    heads = cols // HS
    per_group = heads // GROUPS
    width = per_group * HS
    features = cols * tp
    scale = HS ** (-0.5)
    scale2 = scale * LOG2E
    hp = stat_own.shape[1]
    s = lax.axis_index("section")
    t = lax.axis_index("tp")
    odd = lax.rem(s, 2) == 1
    even = lax.rem(s, 2) == 0

    def copy(src, dst, send, recv, section):
        return pltpu.make_async_remote_copy(
            src_ref=src,
            dst_ref=dst,
            send_sem=send,
            recv_sem=recv,
            device_id={"section": section},
            device_id_type=MESH,
        )

    def group_cols(g):
        return pl.ds(pl.multiple_of(g * width, HS), width)

    def head_cols(h):
        return pl.ds(pl.multiple_of(h * HS, HS), HS)

    near = [(-1, s >= 1), (-2, s >= 2), (1, s + 1 < n), (2, s + 2 < n)]

    barrier = pltpu.get_barrier_semaphore()
    for step, there in near:
        @pl.when(there)
        def _():
            pl.semaphore_signal(
                barrier, inc=1, device_id={"section": s + step}, device_id_type=MESH
            )
    for j in range(1, tp):
        pl.semaphore_signal(
            barrier, inc=1, device_id={"tp": lax.rem(t + j, tp)}, device_id_type=MESH
        )
    pl.semaphore_wait(barrier, jnp.minimum(s, 2) + jnp.minimum(n - 1 - s, 2) + tp - 1)

    doc_own[...] = jnp.broadcast_to(doc_ref[...], doc_own.shape)
    back = [2, 3, 0, 1]

    def doc_copy(i):
        return copy(
            doc_own, doc_buf.at[back[i]], doc_send.at[i], doc_recv.at[back[i]], s + near[i][0]
        )

    for i in range(4):
        @pl.when(near[i][1])
        def _():
            doc_copy(i).start()

    kv_src = (k_ref, v_ref)
    qo_src = (q_ref, do_ref)

    def kv_copy(a, slot, g, src, section):
        c = group_cols(g)
        return copy(
            src.at[:, c], kv_buf.at[a, slot, :, c], kv_send.at[a, slot, g],
            kv_recv.at[a, slot, g], section,
        )

    def qo_copy(a, slot, g, src, section):
        c = group_cols(g)
        return copy(
            src.at[:, c], qo_buf.at[a, slot, :, c], qo_send.at[a, slot, g],
            qo_recv.at[a, slot, g], section,
        )

    def kv_start(g):
        for a in range(2):
            @pl.when(even)
            def _():
                kv_copy(a, 0, g, kv_src[a], s + 1).start()

            @pl.when(s + 2 < n)
            def _():
                kv_copy(a, 1, g, kv_src[a], s + 2).start()

    def qo_start(a, g):
        @pl.when(odd)
        def _():
            qo_copy(a, 0, g, qo_src[a], s - 1).start()

        @pl.when(s >= 2)
        def _():
            qo_copy(a, 1, g, qo_src[a], s - 2).start()

    def kv_arrive(g):
        @pl.when(s >= 2)
        def _():
            for a in range(2):
                kv_copy(a, 1, g, kv_src[a], s).wait_recv()

                @pl.when(odd)
                def _():
                    kv_copy(a, 0, g, kv_buf.at[a, 1], s - 1).start()

        @pl.when(s >= 1)
        def _():
            for a in range(2):
                kv_copy(a, 0, g, kv_src[a], s).wait_recv()

    def qo_far_arrive(g):
        @pl.when(s + 2 < n)
        def _():
            for a in range(2):
                qo_copy(a, 1, g, qo_src[a], s).wait_recv()

                @pl.when(even)
                def _():
                    qo_copy(a, 0, g, qo_buf.at[a, 1], s + 1).start()

    def qo_near_arrive(g):
        @pl.when(s + 1 < n)
        def _():
            for a in range(2):
                qo_copy(a, 0, g, qo_src[a], s).wait_recv()

    def loop(count, f):
        lax.fori_loop(0, count, lambda i, c: (f(i), c)[1], 0)

    loop(GROUPS, kv_start)

    for slot in range(2):
        @pl.when(s < slot + 1)
        def _():
            kv_buf[:, slot] = jnp.zeros((2, rows, cols), kv_buf.dtype)
            doc_buf[slot] = jnp.zeros(doc_buf.shape[1:], doc_buf.dtype)

        @pl.when(s + slot + 1 >= n)
        def _():
            qo_buf[:, slot] = jnp.zeros((2, rows, cols), qo_buf.dtype)
            stat_buf[slot] = jnp.zeros(stat_buf.shape[1:], stat_buf.dtype)
            doc_buf[2 + slot] = jnp.zeros(doc_buf.shape[1:], doc_buf.dtype)

    sums[...] = jnp.zeros(sums.shape, sums.dtype)
    stat_col[...] = jnp.zeros(stat_col.shape, stat_col.dtype)

    doc_row = doc_ref[...].astype(jnp.float32)
    doc_col = jnp.transpose(jnp.broadcast_to(doc_row, (HS, rows)))[:, :1]
    for i in range(4):
        @pl.when(near[i][1])
        def _():
            doc_copy(i).wait_send()
            copy(doc_own, doc_buf.at[i], doc_send.at[i], doc_recv.at[i], s).wait_recv()
    down = lax.broadcasted_iota(jnp.int32, (rows, rows), 0)
    across = lax.broadcasted_iota(jnp.int32, (rows, rows), 1)

    def bias(visible):
        return jnp.where(visible, 0.0, HIDDEN)

    same = doc_col == doc_row
    bias_ref[0] = bias(same & (down >= across))
    bias_t_ref[0] = bias(same & (across >= down))
    for i in range(2):
        for ref, slot, where_far in ((bias_ref, i, down < across), (bias_t_ref, i + 2, across < down)):
            other = doc_buf[slot][:1].astype(jnp.float32)
            visible = (doc_col == other) & near[slot][1]
            if i == 1:
                visible = visible & where_far
            ref[i + 1] = bias(visible)

    lane = lax.broadcasted_iota(jnp.int32, (rows, HS), 1)

    def keys_of(j, c):
        return k_ref[:, c] if j == 0 else kv_buf[0, j - 1, :, c]

    def values_of(j, c):
        return v_ref[:, c] if j == 0 else kv_buf[1, j - 1, :, c]

    def forward_head(h):
        c = head_cols(h)
        q = q_ref[:, c]
        scores = [nt_dot(q, keys_of(j, c)) * scale2 + bias_ref[j] for j in range(3)]
        top = jnp.max(
            jnp.maximum(jnp.maximum(scores[0], scores[1]), scores[2]), axis=-1, keepdims=True
        )
        parts = [jnp.exp2(x - top) for x in scores]
        total = jnp.sum(parts[0] + parts[1] + parts[2], axis=-1, keepdims=True)
        recip = 1.0 / total
        att = jnp.zeros((rows, HS), jnp.float32)
        for j in range(3):
            w = (parts[j] * recip).astype(jnp.bfloat16)
            w_ref[h, :, j * rows : (j + 1) * rows] = w
            att = att + nn_dot(w, values_of(j, c))
        att_ref[:, c] = att
        stat_col[0] = jnp.where(lane == h, top + jnp.log2(total), stat_col[0])
        sums[0] += att * att
        sums[1] += cot_ref[:, c].astype(jnp.float32) * gain_ref[:, c] * att

    def forward_group(g):
        kv_arrive(g)
        qo_start(0, g)
        loop(per_group, lambda i: forward_head(g * per_group + i))

    loop(GROUPS, forward_group)

    def sums_copy(j):
        return pltpu.make_async_remote_copy(
            src_ref=sums,
            dst_ref=sums_buf.at[j - 1],
            send_sem=sums_send.at[j - 1],
            recv_sem=sums_recv.at[j - 1],
            device_id={"tp": lax.rem(t + j, tp)},
            device_id_type=MESH,
        )

    for j in range(1, tp):
        sums_copy(j).start()
    squares, inner = sums[0], sums[1]
    for j in range(1, tp):
        sums_copy(j).wait()
        squares = squares + sums_buf[j - 1, 0]
        inner = inner + sums_buf[j - 1, 1]
    inverse = lax.rsqrt(jnp.sum(squares, axis=-1, keepdims=True) / features + 1e-05)
    factor = inverse * inverse * inverse * jnp.sum(inner, axis=-1, keepdims=True) / features
    sums[0] = jnp.broadcast_to(inverse, (rows, HS))
    sums[1] = jnp.broadcast_to(factor, (rows, HS))

    def norm_head(h):
        c = head_cols(h)
        att = att_ref[:, c]
        gain = gain_ref[:, c]
        normed_ref[:, c] = (att * sums[0] * gain).astype(normed_ref.dtype)
        grad = sums[0] * (cot_ref[:, c].astype(jnp.float32) * gain) - att * sums[1]
        grad = grad.astype(do_ref.dtype)
        do_ref[:, c] = grad
        delta = jnp.sum(grad.astype(jnp.float32) * att, axis=-1, keepdims=True)
        stat_col[1] = jnp.where(lane == h, delta, stat_col[1])

    def norm_group(g):
        loop(per_group, lambda i: norm_head(g * per_group + i))
        qo_start(1, g)

    loop(GROUPS, norm_group)
    for i in range(2):
        stat_own[i] = jnp.transpose(stat_col[i])[:hp]

    def stat_copy(slot):
        return copy(
            stat_own, stat_buf.at[slot], stat_send.at[slot], stat_recv.at[slot], s - slot - 1
        )

    for slot in range(2):
        @pl.when(s >= slot + 1)
        def _():
            stat_copy(slot).start()
    for slot in range(2):
        @pl.when(s + slot + 1 < n)
        def _():
            copy(
                stat_own, stat_buf.at[slot], stat_send.at[slot], stat_recv.at[slot], s
            ).wait_recv()

    def query_head(h):
        c = head_cols(h)
        grad = do_ref[:, c]
        delta = jnp.sum(grad.astype(jnp.float32) * att_ref[:, c], axis=-1, keepdims=True)
        dq = jnp.zeros((rows, HS), jnp.float32)
        for j in range(3):
            w = w_ref[h, :, j * rows : (j + 1) * rows].astype(jnp.float32)
            ds = (w * (nt_dot(grad, values_of(j, c)) - delta)).astype(jnp.bfloat16)
            dq = dq + nn_dot(ds, keys_of(j, c))
        dq_ref[:, c] = (dq * scale).astype(dq_ref.dtype)

    def key_terms(h, j):
        c = head_cols(h)
        if j == 0:
            q, grad = q_ref[:, c], do_ref[:, c]
            log_total, delta = stat_own[0, pl.ds(h, 1), :], stat_own[1, pl.ds(h, 1), :]
        else:
            q, grad = qo_buf[0, j - 1, :, c], qo_buf[1, j - 1, :, c]
            log_total = stat_buf[j - 1, 0, pl.ds(h, 1), :]
            delta = stat_buf[j - 1, 1, pl.ds(h, 1), :]
        w = jnp.exp2(nt_dot(k_ref[:, c], q) * scale2 + bias_t_ref[j] - log_total)
        ds = (w * (nt_dot(v_ref[:, c], grad) - delta)).astype(jnp.bfloat16)
        return nn_dot(ds, q), nn_dot(w.astype(jnp.bfloat16), grad)

    def early_head(h):
        c = head_cols(h)
        query_head(h)
        own, far_one = key_terms(h, 0), key_terms(h, 2)
        dk_acc[:, c] = own[0] + far_one[0]
        dv_acc[:, c] = own[1] + far_one[1]

    def late_head(h):
        c = head_cols(h)
        dk, dv = key_terms(h, 1)
        dk_ref[:, c] = ((dk_acc[:, c] + dk) * scale).astype(dk_ref.dtype)
        dv_ref[:, c] = (dv_acc[:, c] + dv).astype(dv_ref.dtype)

    def backward_step(g):
        @pl.when(g < GROUPS)
        def _():
            qo_far_arrive(g)
            loop(per_group, lambda i: early_head(g * per_group + i))

        @pl.when(g >= 1)
        def _():
            qo_near_arrive(g - 1)
            loop(per_group, lambda i: late_head((g - 1) * per_group + i))

    loop(GROUPS + 1, backward_step)

    for slot in range(2):
        @pl.when(s >= slot + 1)
        def _():
            stat_copy(slot).wait_send()

    def sent(g):
        for a in range(2):
            @pl.when(even | (s >= 3))
            def _():
                kv_copy(a, 0, g, kv_src[a], s).wait_send()

            @pl.when(s + 2 < n)
            def _():
                kv_copy(a, 1, g, kv_src[a], s).wait_send()

            @pl.when(odd | (s + 3 < n))
            def _():
                qo_copy(a, 0, g, qo_src[a], s).wait_send()

            @pl.when(s >= 2)
            def _():
                qo_copy(a, 1, g, qo_src[a], s).wait_send()

    loop(GROUPS, sent)


def body(n, tp, queries, keys, values, cotangent, doc_ids, gain):
    rows, cols = queries.shape
    heads = cols // HS
    hp = -(-heads // 8) * 8
    vmem = pl.BlockSpec(memory_space=pltpu.VMEM)
    bf16, f32 = jnp.bfloat16, jnp.float32
    dma = pltpu.SemaphoreType.DMA
    out = jax.ShapeDtypeStruct((rows, cols), bf16)
    return pl.pallas_call(
        functools.partial(kernel, n, tp),
        out_shape=(out,) * 4,
        in_specs=[vmem] * 6,
        out_specs=(vmem,) * 4,
        scratch_shapes=[
            pltpu.VMEM((2, 2, rows, cols), bf16),
            pltpu.VMEM((2, 2, rows, cols), bf16),
            pltpu.VMEM((rows, cols), bf16),
            pltpu.VMEM((rows, cols), f32),
            pltpu.VMEM((heads, rows, 3 * rows), bf16),
            pltpu.VMEM((3, rows, rows), f32),
            pltpu.VMEM((3, rows, rows), f32),
            pltpu.VMEM((rows, cols), f32),
            pltpu.VMEM((rows, cols), f32),
            pltpu.VMEM((8, rows), jnp.int32),
            pltpu.VMEM((4, 8, rows), jnp.int32),
            pltpu.VMEM((2, rows, HS), f32),
            pltpu.VMEM((max(tp - 1, 1), 2, rows, HS), f32),
            pltpu.VMEM((2, rows, HS), f32),
            pltpu.VMEM((2, hp, rows), f32),
            pltpu.VMEM((2, 2, hp, rows), f32),
            dma((2, 2, GROUPS)),
            dma((2, 2, GROUPS)),
            dma((2, 2, GROUPS)),
            dma((2, 2, GROUPS)),
            dma((4,)),
            dma((4,)),
            dma((max(tp - 1, 1),)),
            dma((max(tp - 1, 1),)),
            dma((2,)),
            dma((2,)),
        ],
        compiler_params=pltpu.CompilerParams(
            collective_id=0, has_side_effects=True, vmem_limit_bytes=60 * 1024 * 1024
        ),
        cost_estimate=pl.CostEstimate(
            flops=16 * heads * 3 * rows * rows * HS,
            bytes_accessed=16 * rows * cols,
            transcendentals=6 * heads * rows * rows,
        ),
    )(queries, keys, values, cotangent, doc_ids.reshape(1, rows), gain.reshape(1, cols))


def solution(mesh):
    wide = P("section", "tp")
    return jax.shard_map(
        functools.partial(body, mesh.shape["section"], mesh.shape["tp"]),
        mesh=mesh,
        in_specs=(wide, wide, wide, wide, P("section"), P("tp")),
        out_specs=(wide,) * 4,
        check_vma=False,
    )
```

time: 455 us -> 232 us (0.51)
  waiting for transfers between devices: 270 us -> 0 us
  Pallas kernels: 0 us -> 222 us
  matrix products: 69.1 us -> 0 us
  other arithmetic: 35.8 us -> 0 us
  local copies, waits for them, and re-layouts: 43.6 us -> 9.4 us
  starting transfers between devices: 32.3 us -> 0 us
    ppermute x10 -> x0, waiting for transfers between devices: 270 us -> none  [from_behind(): lax.ppermute(value, axis, [(source, source + steps) for source in range(i...]
    pallas_call x0 -> x1, Pallas kernels: none -> 222 us  [body(): pl.pallas_call(functools.partial(kernel, n, tp), out_shape=(out,) * 4, in...]
    dot_general x6 -> x0, matrix products: 69.1 us -> none  [the longest x1 16.1 us: body(): jnp.einsum('qhd,khd->hqk', grad_heads, value_band, preferred_element_type...]
    ppermute x10 -> x0, starting transfers between devices: 32.3 us -> none  [from_behind(): lax.ppermute(value, axis, [(source, source + steps) for source in range(i...]
    slice x8 -> x0, local copies, waits for them, and re-layouts: 28.6 us -> none  [the longest x3 12.3 us: body(): key_terms[distance * tok_rows:(distance + 1) * tok_rows]]
    reduce_sum x3 -> x0, other arithmetic: 13.7 us -> none  [the longest x1 8.96 us: body(): jnp.sum(jnp.exp(scores - row_max), axis=-1, keepdims=True)]
    convert_element_type x3 -> x0, other arithmetic: 13 us -> none  [the longest x1 4.66 us: body(): grad_key.astype(jnp.bfloat16)]
    concatenate x4 -> x0, other arithmetic: 4.95 us -> none  [the longest x1 2.13 us: body(): jnp.concatenate([entry[1] for entry in blocks], 0)]
  transfers between devices with their start and end apart: 10 -> 0, of which waited for: 6 -> 0; matrix products, arithmetic and copies ran while one was open for 13% -> 0% of each run, Pallas kernels for 0% -> 0%
where the time goes in v1:
time: 232 us
  Pallas kernels  222 us (96%)
  local copies, waits for them, and re-layouts  9.4 us (4%)
    pallas_call x1, Pallas kernels, body(): pl.pallas_call(functools.partial(kernel, n, tp), out_shape=(out,) * 4, in...  222 us
    unnamed x10, local copies, waits for them, and re-layouts  6.86 us

profile of v1, /device:TPU:14, one launch (start us, length us, event | category | flops | bytes accessed | tf_op | source)
XLA Modules:
  0.0 232.0 jit_solution(6420183847182989975)
XLA Ops:
  0.6 1.2 reshape.14.doc_ref
  1.9 1.3 reshape.15.gain_ref
  3.2 221.9 %shard_map.93 = (bf16[384,1536]{1,0:T(8,128)(2,1)}, bf16[384,1536]{1,0:T(8,128)(2,1)}, bf16[384,1536]{1,0:T(8,128)(2,1)}, bf16[384,1536]{1,0:T(8,128)(2,1)}) custom-call(bf16[384,1536]{1,0:T(8,128)(2,1)} %q_ref.1, bf16[384,1536]{1,0:T(8,128)(2,1)} %k_ref.1, bf16[384,1536]{1,0:T(8,128)(2,1)} %v_ref.1, bf16[384,1536]{1,0:T(8,128)(2,1)} %cot_ref.1, ...), custom_call_target="tpu_custom_call" | custom-call | flops 10871635968 | bytes 9437184 | tf_op jit(solution)/shard_map/pallas_call | solution.py:411
  225.1 0.0 copy-start.2
  225.1 2.5 %copy.14 = bf16[384,1536]{1,0:T(8,128)(2,1)} copy(bf16[384,1536]{1,0:T(8,128)(2,1)} %get-tuple-element.8) | data formatting | bytes 2359296
  227.6 0.0 copy-done.2
  227.6 0.0 copy-start.1
  227.6 1.0 copy.15
  228.6 0.7 copy-done.1
  229.3 0.0 copy-start
  229.3 1.0 copy.16
  230.3 0.7 copy-done
  231.0 1.0 copy.17
Async XLA Ops:
  225.1 2.5 %copy-start.2 = (bf16[384,1536]{1,0:T(8,128)(2,1)S(1)}, bf16[384,1536]{1,0:T(8,128)(2,1)}, u32[]{:S(2)}) copy-start(bf16[384,1536]{1,0:T(8,128)(2,1)} %get-tuple-element.9) | copy-start | bytes 3538948
  227.6 1.7 copy-start.1
  229.3 1.7 copy-start

commit v2 on v1

--- a/solution.py
+++ b/solution.py
@@ -9,7 +9,7 @@
 from jax.sharding import PartitionSpec as P
 
 HS = 128
-GROUPS = 4
+GROUPS = 6
 MESH = pl.DeviceIdType.MESH
 LOG2E = math.log2(math.e)
 HIDDEN = -1e30
@@ -172,15 +172,14 @@
             for a in range(2):
                 kv_copy(a, 0, g, kv_src[a], s).wait_recv()
 
-    def qo_far_arrive(g):
-        @pl.when(s + 2 < n)
-        def _():
-            for a in range(2):
-                qo_copy(a, 1, g, qo_src[a], s).wait_recv()
-
-                @pl.when(even)
-                def _():
-                    qo_copy(a, 0, g, qo_buf.at[a, 1], s + 1).start()
+    def qo_far_arrive(a, g):
+        @pl.when((s + 2 < n) & (g >= 0) & (g < GROUPS))
+        def _():
+            qo_copy(a, 1, g, qo_src[a], s).wait_recv()
+
+            @pl.when(even)
+            def _():
+                qo_copy(a, 0, g, qo_buf.at[a, 1], s + 1).start()
 
     def qo_near_arrive(g):
         @pl.when(s + 1 < n)
@@ -218,42 +217,46 @@
     down = lax.broadcasted_iota(jnp.int32, (rows, rows), 0)
     across = lax.broadcasted_iota(jnp.int32, (rows, rows), 1)
 
+    spans = (slice(0, rows), slice(rows, 3 * rows))
+
     def bias(visible):
         return jnp.where(visible, 0.0, HIDDEN)
 
     same = doc_col == doc_row
-    bias_ref[0] = bias(same & (down >= across))
-    bias_t_ref[0] = bias(same & (across >= down))
+    bias_ref[:, spans[0]] = bias(same & (down >= across))
+    bias_t_ref[:, spans[0]] = bias(same & (across >= down))
     for i in range(2):
         for ref, slot, where_far in ((bias_ref, i, down < across), (bias_t_ref, i + 2, across < down)):
             other = doc_buf[slot][:1].astype(jnp.float32)
             visible = (doc_col == other) & near[slot][1]
             if i == 1:
                 visible = visible & where_far
-            ref[i + 1] = bias(visible)
+            ref[:, (i + 1) * rows : (i + 2) * rows] = bias(visible)
 
     lane = lax.broadcasted_iota(jnp.int32, (rows, HS), 1)
 
     def keys_of(j, c):
-        return k_ref[:, c] if j == 0 else kv_buf[0, j - 1, :, c]
+        return k_ref[:, c] if j == 0 else kv_buf[0, :, :, c].reshape(2 * rows, HS)
 
     def values_of(j, c):
-        return v_ref[:, c] if j == 0 else kv_buf[1, j - 1, :, c]
+        return v_ref[:, c] if j == 0 else kv_buf[1, :, :, c].reshape(2 * rows, HS)
 
     def forward_head(h):
         c = head_cols(h)
         q = q_ref[:, c]
-        scores = [nt_dot(q, keys_of(j, c)) * scale2 + bias_ref[j] for j in range(3)]
-        top = jnp.max(
-            jnp.maximum(jnp.maximum(scores[0], scores[1]), scores[2]), axis=-1, keepdims=True
+        scores = [nt_dot(q, keys_of(j, c)) * scale2 + bias_ref[:, spans[j]] for j in range(2)]
+        top = jnp.maximum(
+            jnp.max(scores[0], axis=-1, keepdims=True), jnp.max(scores[1], axis=-1, keepdims=True)
         )
         parts = [jnp.exp2(x - top) for x in scores]
-        total = jnp.sum(parts[0] + parts[1] + parts[2], axis=-1, keepdims=True)
+        total = jnp.sum(parts[0], axis=-1, keepdims=True) + jnp.sum(
+            parts[1], axis=-1, keepdims=True
+        )
         recip = 1.0 / total
         att = jnp.zeros((rows, HS), jnp.float32)
-        for j in range(3):
+        for j in range(2):
             w = (parts[j] * recip).astype(jnp.bfloat16)
-            w_ref[h, :, j * rows : (j + 1) * rows] = w
+            w_ref[h, :, spans[j]] = w
             att = att + nn_dot(w, values_of(j, c))
         att_ref[:, c] = att
         stat_col[0] = jnp.where(lane == h, top + jnp.log2(total), stat_col[0])
@@ -262,7 +265,11 @@
 
     def forward_group(g):
         kv_arrive(g)
-        qo_start(0, g)
+
+        @pl.when(g == GROUPS - 1)
+        def _():
+            loop(GROUPS, lambda i: qo_start(0, i))
+
         loop(per_group, lambda i: forward_head(g * per_group + i))
 
     loop(GROUPS, forward_group)
@@ -279,6 +286,8 @@
 
     for j in range(1, tp):
         sums_copy(j).start()
+    for g in range(2):
+        qo_far_arrive(0, g)
     squares, inner = sums[0], sums[1]
     for j in range(1, tp):
         sums_copy(j).wait()
@@ -317,6 +326,49 @@
         @pl.when(s >= slot + 1)
         def _():
             stat_copy(slot).start()
+    def query_head(h):
+        c = head_cols(h)
+        grad = do_ref[:, c]
+        delta = jnp.sum(grad.astype(jnp.float32) * att_ref[:, c], axis=-1, keepdims=True)
+        dq = jnp.zeros((rows, HS), jnp.float32)
+        for j in range(2):
+            w = w_ref[h, :, spans[j]].astype(jnp.float32)
+            ds = (w * (nt_dot(grad, values_of(j, c)) - delta)).astype(jnp.bfloat16)
+            dq = dq + nn_dot(ds, keys_of(j, c))
+        dq_ref[:, c] = (dq * scale).astype(dq_ref.dtype)
+
+    def key_terms(h, q, grad, mask, log_total, delta):
+        c = head_cols(h)
+        w = jnp.exp2(nt_dot(k_ref[:, c], q) * scale2 + mask - log_total)
+        ds = (w * (nt_dot(v_ref[:, c], grad) - delta)).astype(jnp.bfloat16)
+        return nn_dot(ds, q), nn_dot(w.astype(jnp.bfloat16), grad)
+
+    def local_head(h):
+        c = head_cols(h)
+        query_head(h)
+        log_total, delta = [stat_own[i, pl.ds(h, 1), :] for i in range(2)]
+        dk, dv = key_terms(h, q_ref[:, c], do_ref[:, c], bias_t_ref[:, spans[0]], log_total, delta)
+        dk_acc[:, c] = dk
+        dv_acc[:, c] = dv
+
+    def remote_head(h):
+        c = head_cols(h)
+        q, grad = [qo_buf[a, :, :, c].reshape(2 * rows, HS) for a in range(2)]
+        log_total, delta = [
+            jnp.concatenate([stat_buf[j, i, pl.ds(h, 1), :] for j in range(2)], axis=1)
+            for i in range(2)
+        ]
+        dk, dv = key_terms(h, q, grad, bias_t_ref[:, spans[1]], log_total, delta)
+        dk_ref[:, c] = ((dk_acc[:, c] + dk) * scale).astype(dk_ref.dtype)
+        dv_ref[:, c] = (dv_acc[:, c] + dv).astype(dv_ref.dtype)
+
+    def local_group(g):
+        loop(per_group, lambda i: local_head(g * per_group + i))
+        qo_far_arrive(0, g + 2)
+        qo_far_arrive(1, g - 2)
+
+    loop(GROUPS, local_group)
+
     for slot in range(2):
         @pl.when(s + slot + 1 < n)
         def _():
@@ -324,55 +376,13 @@
                 stat_own, stat_buf.at[slot], stat_send.at[slot], stat_recv.at[slot], s
             ).wait_recv()
 
-    def query_head(h):
-        c = head_cols(h)
-        grad = do_ref[:, c]
-        delta = jnp.sum(grad.astype(jnp.float32) * att_ref[:, c], axis=-1, keepdims=True)
-        dq = jnp.zeros((rows, HS), jnp.float32)
-        for j in range(3):
-            w = w_ref[h, :, j * rows : (j + 1) * rows].astype(jnp.float32)
-            ds = (w * (nt_dot(grad, values_of(j, c)) - delta)).astype(jnp.bfloat16)
-            dq = dq + nn_dot(ds, keys_of(j, c))
-        dq_ref[:, c] = (dq * scale).astype(dq_ref.dtype)
-
-    def key_terms(h, j):
-        c = head_cols(h)
-        if j == 0:
-            q, grad = q_ref[:, c], do_ref[:, c]
-            log_total, delta = stat_own[0, pl.ds(h, 1), :], stat_own[1, pl.ds(h, 1), :]
-        else:
-            q, grad = qo_buf[0, j - 1, :, c], qo_buf[1, j - 1, :, c]
-            log_total = stat_buf[j - 1, 0, pl.ds(h, 1), :]
-            delta = stat_buf[j - 1, 1, pl.ds(h, 1), :]
-        w = jnp.exp2(nt_dot(k_ref[:, c], q) * scale2 + bias_t_ref[j] - log_total)
-        ds = (w * (nt_dot(v_ref[:, c], grad) - delta)).astype(jnp.bfloat16)
-        return nn_dot(ds, q), nn_dot(w.astype(jnp.bfloat16), grad)
-
-    def early_head(h):
-        c = head_cols(h)
-        query_head(h)
-        own, far_one = key_terms(h, 0), key_terms(h, 2)
-        dk_acc[:, c] = own[0] + far_one[0]
-        dv_acc[:, c] = own[1] + far_one[1]
-
-    def late_head(h):
-        c = head_cols(h)
-        dk, dv = key_terms(h, 1)
-        dk_ref[:, c] = ((dk_acc[:, c] + dk) * scale).astype(dk_ref.dtype)
-        dv_ref[:, c] = (dv_acc[:, c] + dv).astype(dv_ref.dtype)
-
-    def backward_step(g):
-        @pl.when(g < GROUPS)
-        def _():
-            qo_far_arrive(g)
-            loop(per_group, lambda i: early_head(g * per_group + i))
-
-        @pl.when(g >= 1)
-        def _():
-            qo_near_arrive(g - 1)
-            loop(per_group, lambda i: late_head((g - 1) * per_group + i))
-
-    loop(GROUPS + 1, backward_step)
+
+    def remote_group(g):
+        qo_far_arrive(1, g + GROUPS - 2)
+        qo_near_arrive(g)
+        loop(per_group, lambda i: remote_head(g * per_group + i))
+
+    loop(GROUPS, remote_group)
 
     for slot in range(2):
         @pl.when(s >= slot + 1)
@@ -419,8 +429,8 @@
             pltpu.VMEM((rows, cols), bf16),
             pltpu.VMEM((rows, cols), f32),
             pltpu.VMEM((heads, rows, 3 * rows), bf16),
-            pltpu.VMEM((3, rows, rows), f32),
-            pltpu.VMEM((3, rows, rows), f32),
+            pltpu.VMEM((rows, 3 * rows), f32),
+            pltpu.VMEM((rows, 3 * rows), f32),
             pltpu.VMEM((rows, cols), f32),
             pltpu.VMEM((rows, cols), f32),
             pltpu.VMEM((8, rows), jnp.int32),

time: 232 us -> 189 us (0.81)
  Pallas kernels: 222 us -> 178 us
    pallas_call x1, Pallas kernels: 222 us -> 178 us  [body(): pl.pallas_call(functools.partial(kernel, n, tp), out_shape=(out,) * 4, in...]
where the time goes in v2:
time: 189 us; the launch traced here: 188 us
  Pallas kernels  178 us (94%)
  local copies, waits for them, and re-layouts  9.4 us (5%)
    pallas_call x1, Pallas kernels, body(): pl.pallas_call(functools.partial(kernel, n, tp), out_shape=(out,) * 4, in...  178 us
    unnamed x10, local copies, waits for them, and re-layouts  6.86 us

profile of v2, /device:TPU:14, one launch (start us, length us, event | category | flops | bytes accessed | tf_op | source)
XLA Modules:
  0.0 187.8 jit_solution(15566404867798432540)
XLA Ops:
  0.6 1.2 reshape.14.doc_ref
  1.9 1.3 reshape.15.gain_ref
  3.2 177.8 %shard_map.93 = (bf16[384,1536]{1,0:T(8,128)(2,1)}, bf16[384,1536]{1,0:T(8,128)(2,1)}, bf16[384,1536]{1,0:T(8,128)(2,1)}, bf16[384,1536]{1,0:T(8,128)(2,1)}) custom-call(bf16[384,1536]{1,0:T(8,128)(2,1)} %q_ref.1, bf16[384,1536]{1,0:T(8,128)(2,1)} %k_ref.1, bf16[384,1536]{1,0:T(8,128)(2,1)} %v_ref.1, bf16[384,1536]{1,0:T(8,128)(2,1)} %cot_ref.1, ...), custom_call_target="tpu_custom_call" | custom-call | flops 10871635968 | bytes 9437184 | tf_op jit(solution)/shard_map/pallas_call | solution.py:421
  180.9 0.0 copy-start.2
  181.0 2.5 %copy.14 = bf16[384,1536]{1,0:T(8,128)(2,1)} copy(bf16[384,1536]{1,0:T(8,128)(2,1)} %get-tuple-element.8) | data formatting | bytes 2359296
  183.4 0.0 copy-done.2
  183.4 0.0 copy-start.1
  183.4 1.0 copy.15
  184.4 0.7 copy-done.1
  185.1 0.0 copy-start
  185.1 1.0 copy.16
  186.1 0.7 copy-done
  186.8 1.0 copy.17
Async XLA Ops:
  180.9 2.5 %copy-start.2 = (bf16[384,1536]{1,0:T(8,128)(2,1)S(1)}, bf16[384,1536]{1,0:T(8,128)(2,1)}, u32[]{:S(2)}) copy-start(bf16[384,1536]{1,0:T(8,128)(2,1)} %get-tuple-element.9) | copy-start | bytes 3538948
  183.4 1.7 copy-start.1
  185.1 1.7 copy-start

commit v3 on v2

--- a/solution.py
+++ b/solution.py
@@ -10,6 +10,7 @@
 
 HS = 128
 GROUPS = 6
+AHEAD = 3
 MESH = pl.DeviceIdType.MESH
 LOG2E = math.log2(math.e)
 HIDDEN = -1e30
@@ -138,48 +139,65 @@
             qo_recv.at[a, slot, g], section,
         )
 
-    def kv_start(g):
+    first = lax.rem(t, 2) == 0
+    second = lax.rem(t, 2) == 1
+
+    def in_turn(one, other):
+        pl.when(one[0] & first)(lambda: one[1]())
+        pl.when(other[0])(lambda: other[1]())
+        pl.when(one[0] & second)(lambda: one[1]())
+
+    def kv_start(a, g):
+        in_turn(
+            (even, lambda: kv_copy(a, 0, g, kv_src[a], s + 1).start()),
+            (s + 2 < n, lambda: kv_copy(a, 1, g, kv_src[a], s + 2).start()),
+        )
+
+    def kv_arrive(a, g):
+        @pl.when(s >= 2)
+        def _():
+            kv_copy(a, 1, g, kv_src[a], s).wait_recv()
+
+        more = odd & (s + 2 < n) & (g + 1 < GROUPS)
+        in_turn(
+            (odd & (s >= 3), lambda: kv_copy(a, 0, g, kv_buf.at[a, 1], s - 1).start()),
+            (more, lambda: kv_copy(a, 1, g + 1, kv_src[a], s + 2).start()),
+        )
+
+    def kv_near_arrive(a, g):
+        @pl.when(s >= 1)
+        def _():
+            kv_copy(a, 0, g, kv_src[a], s).wait_recv()
+
+    def stream(i, f):
         for a in range(2):
-            @pl.when(even)
-            def _():
-                kv_copy(a, 0, g, kv_src[a], s + 1).start()
-
-            @pl.when(s + 2 < n)
-            def _():
-                kv_copy(a, 1, g, kv_src[a], s + 2).start()
-
-    def qo_start(a, g):
-        @pl.when(odd)
-        def _():
-            qo_copy(a, 0, g, qo_src[a], s - 1).start()
-
-        @pl.when(s >= 2)
-        def _():
-            qo_copy(a, 1, g, qo_src[a], s - 2).start()
-
-    def kv_arrive(g):
-        @pl.when(s >= 2)
-        def _():
-            for a in range(2):
-                kv_copy(a, 1, g, kv_src[a], s).wait_recv()
-
-                @pl.when(odd)
-                def _():
-                    kv_copy(a, 0, g, kv_buf.at[a, 1], s - 1).start()
-
-        @pl.when(s >= 1)
-        def _():
-            for a in range(2):
-                kv_copy(a, 0, g, kv_src[a], s).wait_recv()
-
-    def qo_far_arrive(a, g):
-        @pl.when((s + 2 < n) & (g >= 0) & (g < GROUPS))
-        def _():
-            qo_copy(a, 1, g, qo_src[a], s).wait_recv()
-
-            @pl.when(even)
-            def _():
-                qo_copy(a, 0, g, qo_buf.at[a, 1], s + 1).start()
+            pl.when((i >= a * GROUPS) & (i < (a + 1) * GROUPS))(lambda: f(a, i - a * GROUPS))
+
+    def qo_start(i):
+        def start(a, g):
+            in_turn(
+                (odd, lambda: qo_copy(a, 0, g, qo_src[a], s - 1).start()),
+                (s >= 2, lambda: qo_copy(a, 1, g, qo_src[a], s - 2).start()),
+            )
+
+        stream(i, start)
+
+    def qo_pass(k):
+        passes = even & (s + 2 < n)
+
+        @pl.when(s + 2 < n)
+        def _():
+            stream(k, lambda a, g: qo_copy(a, 1, g, qo_src[a], s).wait_recv())
+
+        in_turn(
+            (
+                passes,
+                lambda: stream(
+                    k, lambda a, g: qo_copy(a, 0, g, qo_buf.at[a, 1], s + 1).start()
+                ),
+            ),
+            (k + AHEAD >= 0, lambda: qo_start(k + AHEAD)),
+        )
 
     def qo_near_arrive(g):
         @pl.when(s + 1 < n)
@@ -190,7 +208,13 @@
     def loop(count, f):
         lax.fori_loop(0, count, lambda i, c: (f(i), c)[1], 0)
 
-    loop(GROUPS, kv_start)
+    def kv_first(g):
+        @pl.when(even | (g == 0))
+        def _():
+            for a in range(2):
+                kv_start(a, g)
+
+    loop(GROUPS, kv_first)
 
     for slot in range(2):
         @pl.when(s < slot + 1)
@@ -264,11 +288,14 @@
         sums[1] += cot_ref[:, c].astype(jnp.float32) * gain_ref[:, c] * att
 
     def forward_group(g):
-        kv_arrive(g)
+        for a in range(2):
+            kv_arrive(a, g)
+        for a in range(2):
+            kv_near_arrive(a, g)
 
         @pl.when(g == GROUPS - 1)
         def _():
-            loop(GROUPS, lambda i: qo_start(0, i))
+            qo_start(0)
 
         loop(per_group, lambda i: forward_head(g * per_group + i))
 
@@ -286,8 +313,8 @@
 
     for j in range(1, tp):
         sums_copy(j).start()
-    for g in range(2):
-        qo_far_arrive(0, g)
+    for i in range(1, AHEAD):
+        qo_start(i)
     squares, inner = sums[0], sums[1]
     for j in range(1, tp):
         sums_copy(j).wait()
@@ -311,7 +338,6 @@
 
     def norm_group(g):
         loop(per_group, lambda i: norm_head(g * per_group + i))
-        qo_start(1, g)
 
     loop(GROUPS, norm_group)
     for i in range(2):
@@ -362,12 +388,17 @@
         dk_ref[:, c] = ((dk_acc[:, c] + dk) * scale).astype(dk_ref.dtype)
         dv_ref[:, c] = (dv_acc[:, c] + dv).astype(dv_ref.dtype)
 
+    for k in range(2):
+        qo_pass(k)
+
     def local_group(g):
-        loop(per_group, lambda i: local_head(g * per_group + i))
-        qo_far_arrive(0, g + 2)
-        qo_far_arrive(1, g - 2)
-
-    loop(GROUPS, local_group)
+        for i in range(per_group):
+            local_head(g * per_group + i)
+            if i < 2:
+                qo_pass(2 * g + 2 + i)
+
+    half = GROUPS // 2
+    loop(half, local_group)
 
     for slot in range(2):
         @pl.when(s + slot + 1 < n)
@@ -376,13 +407,15 @@
                 stat_own, stat_buf.at[slot], stat_send.at[slot], stat_recv.at[slot], s
             ).wait_recv()
 
-
     def remote_group(g):
-        qo_far_arrive(1, g + GROUPS - 2)
         qo_near_arrive(g)
         loop(per_group, lambda i: remote_head(g * per_group + i))
 
-    loop(GROUPS, remote_group)
+    def both_groups(i):
+        local_group(half + i)
+        loop(2, lambda j: remote_group(2 * i + j))
+
+    loop(half, both_groups)
 
     for slot in range(2):
         @pl.when(s >= slot + 1)

time: 189 us -> 229 us (1.21)
  the two profiles are of different devices: /device:TPU:14 before, /device:TPU:22 now
where the time goes in v3:
time: 229 us
  Pallas kernels  219 us (96%)
  local copies, waits for them, and re-layouts  9.4 us (4%)
    pallas_call x1, Pallas kernels, body(): pl.pallas_call(functools.partial(kernel, n, tp), out_shape=(out,) * 4, in...  219 us
    unnamed x10, local copies, waits for them, and re-layouts  6.86 us

profile of v3, /device:TPU:22, one launch (start us, length us, event | category | flops | bytes accessed | tf_op | source)
XLA Modules:
  0.0 228.9 jit_solution(10671955636926237072)
XLA Ops:
  0.6 1.2 reshape.14.doc_ref
  1.9 1.3 reshape.15.gain_ref
  3.2 218.8 %shard_map.93 = (bf16[384,1536]{1,0:T(8,128)(2,1)}, bf16[384,1536]{1,0:T(8,128)(2,1)}, bf16[384,1536]{1,0:T(8,128)(2,1)}, bf16[384,1536]{1,0:T(8,128)(2,1)}) custom-call(bf16[384,1536]{1,0:T(8,128)(2,1)} %q_ref.1, bf16[384,1536]{1,0:T(8,128)(2,1)} %k_ref.1, bf16[384,1536]{1,0:T(8,128)(2,1)} %v_ref.1, bf16[384,1536]{1,0:T(8,128)(2,1)} %cot_ref.1, ...), custom_call_target="tpu_custom_call" | custom-call | flops 10871635968 | bytes 9437184 | tf_op jit(solution)/shard_map/pallas_call | solution.py:454
  222.0 0.0 copy-start.2
  222.0 2.5 %copy.14 = bf16[384,1536]{1,0:T(8,128)(2,1)} copy(bf16[384,1536]{1,0:T(8,128)(2,1)} %get-tuple-element.8) | data formatting | bytes 2359296
  224.5 0.0 copy-done.2
  224.5 0.0 copy-start.1
  224.5 1.0 copy.15
  225.5 0.7 copy-done.1
  226.2 0.0 copy-start
  226.2 1.0 copy.16
  227.2 0.7 copy-done
  227.9 1.0 copy.17
Async XLA Ops:
  222.0 2.5 %copy-start.2 = (bf16[384,1536]{1,0:T(8,128)(2,1)S(1)}, bf16[384,1536]{1,0:T(8,128)(2,1)}, u32[]{:S(2)}) copy-start(bf16[384,1536]{1,0:T(8,128)(2,1)} %get-tuple-element.9) | copy-start | bytes 3538948
  224.5 1.7 copy-start.1
  226.2 1.7 copy-start

commit v4 on v3

--- a/solution.py
+++ b/solution.py
@@ -10,7 +10,8 @@
 
 HS = 128
 GROUPS = 6
-AHEAD = 3
+DEPTH = 2
+AHEAD = 4
 MESH = pl.DeviceIdType.MESH
 LOG2E = math.log2(math.e)
 HIDDEN = -1e30
@@ -153,16 +154,27 @@
             (s + 2 < n, lambda: kv_copy(a, 1, g, kv_src[a], s + 2).start()),
         )
 
-    def kv_arrive(a, g):
+    def kv_pass(a, g):
         @pl.when(s >= 2)
         def _():
             kv_copy(a, 1, g, kv_src[a], s).wait_recv()
 
-        more = odd & (s + 2 < n) & (g + 1 < GROUPS)
-        in_turn(
-            (odd & (s >= 3), lambda: kv_copy(a, 0, g, kv_buf.at[a, 1], s - 1).start()),
-            (more, lambda: kv_copy(a, 1, g + 1, kv_src[a], s + 2).start()),
-        )
+            @pl.when(odd)
+            def _():
+                kv_copy(a, 0, g, kv_buf.at[a, 1], s - 1).start()
+
+    def kv_next(a, g):
+        @pl.when(even)
+        def _():
+            kv_copy(a, 0, g, kv_src[a], s).wait_send()
+
+        @pl.when(s + 2 < n)
+        def _():
+            kv_copy(a, 1, g, kv_src[a], s).wait_send()
+
+        @pl.when(g + DEPTH < GROUPS)
+        def _():
+            kv_start(a, g + DEPTH)
 
     def kv_near_arrive(a, g):
         @pl.when(s >= 1)
@@ -189,15 +201,19 @@
         def _():
             stream(k, lambda a, g: qo_copy(a, 1, g, qo_src[a], s).wait_recv())
 
-        in_turn(
-            (
-                passes,
-                lambda: stream(
-                    k, lambda a, g: qo_copy(a, 0, g, qo_buf.at[a, 1], s + 1).start()
-                ),
-            ),
-            (k + AHEAD >= 0, lambda: qo_start(k + AHEAD)),
-        )
+        pl.when(passes)(
+            lambda: stream(k, lambda a, g: qo_copy(a, 0, g, qo_buf.at[a, 1], s + 1).start())
+        )
+
+        @pl.when(odd)
+        def _():
+            stream(k, lambda a, g: qo_copy(a, 0, g, qo_src[a], s).wait_send())
+
+        @pl.when(s >= 2)
+        def _():
+            stream(k, lambda a, g: qo_copy(a, 1, g, qo_src[a], s).wait_send())
+
+        qo_start(k + AHEAD)
 
     def qo_near_arrive(g):
         @pl.when(s + 1 < n)
@@ -208,13 +224,9 @@
     def loop(count, f):
         lax.fori_loop(0, count, lambda i, c: (f(i), c)[1], 0)
 
-    def kv_first(g):
-        @pl.when(even | (g == 0))
-        def _():
-            for a in range(2):
-                kv_start(a, g)
-
-    loop(GROUPS, kv_first)
+    for g in range(DEPTH):
+        for a in range(2):
+            kv_start(a, g)
 
     for slot in range(2):
         @pl.when(s < slot + 1)
@@ -289,13 +301,16 @@
 
     def forward_group(g):
         for a in range(2):
-            kv_arrive(a, g)
+            kv_pass(a, g)
+        for a in range(2):
+            kv_next(a, g)
         for a in range(2):
             kv_near_arrive(a, g)
 
         @pl.when(g == GROUPS - 1)
         def _():
-            qo_start(0)
+            for k in range(AHEAD):
+                qo_start(k)
 
         loop(per_group, lambda i: forward_head(g * per_group + i))
 
@@ -313,8 +328,6 @@
 
     for j in range(1, tp):
         sums_copy(j).start()
-    for i in range(1, AHEAD):
-        qo_start(i)
     squares, inner = sums[0], sums[1]
     for j in range(1, tp):
         sums_copy(j).wait()
@@ -424,21 +437,13 @@
 
     def sent(g):
         for a in range(2):
-            @pl.when(even | (s >= 3))
+            @pl.when(odd & (s >= 3))
             def _():
                 kv_copy(a, 0, g, kv_src[a], s).wait_send()
 
-            @pl.when(s + 2 < n)
-            def _():
-                kv_copy(a, 1, g, kv_src[a], s).wait_send()
-
-            @pl.when(odd | (s + 3 < n))
+            @pl.when(even & (s + 2 < n))
             def _():
                 qo_copy(a, 0, g, qo_src[a], s).wait_send()
-
-            @pl.when(s >= 2)
-            def _():
-                qo_copy(a, 1, g, qo_src[a], s).wait_send()
 
     loop(GROUPS, sent)
 

time: 229 us -> 227 us (level)
  the two profiles are of different devices: /device:TPU:22 before, /device:TPU:14 now
where the time goes in v4:
time: 227 us
  Pallas kernels  217 us (96%)
  local copies, waits for them, and re-layouts  9.4 us (4%)
    pallas_call x1, Pallas kernels, body(): pl.pallas_call(functools.partial(kernel, n, tp), out_shape=(out,) * 4, in...  217 us
    unnamed x10, local copies, waits for them, and re-layouts  6.86 us

profile of v4, /device:TPU:14, one launch (start us, length us, event | category | flops | bytes accessed | tf_op | source)
XLA Modules:
  0.0 227.1 jit_solution(15193460863525600777)
XLA Ops:
  0.6 1.2 reshape.14.doc_ref
  1.9 1.3 reshape.15.gain_ref
  3.2 217.1 %shard_map.93 = (bf16[384,1536]{1,0:T(8,128)(2,1)}, bf16[384,1536]{1,0:T(8,128)(2,1)}, bf16[384,1536]{1,0:T(8,128)(2,1)}, bf16[384,1536]{1,0:T(8,128)(2,1)}) custom-call(bf16[384,1536]{1,0:T(8,128)(2,1)} %q_ref.1, bf16[384,1536]{1,0:T(8,128)(2,1)} %k_ref.1, bf16[384,1536]{1,0:T(8,128)(2,1)} %v_ref.1, bf16[384,1536]{1,0:T(8,128)(2,1)} %cot_ref.1, ...), custom_call_target="tpu_custom_call" | custom-call | flops 10871635968 | bytes 9437184 | tf_op jit(solution)/shard_map/pallas_call | solution.py:459
  220.3 0.0 copy-start.2
  220.3 2.5 %copy.14 = bf16[384,1536]{1,0:T(8,128)(2,1)} copy(bf16[384,1536]{1,0:T(8,128)(2,1)} %get-tuple-element.8) | data formatting | bytes 2359296
  222.7 0.0 copy-done.2
  222.7 0.0 copy-start.1
  222.7 1.0 copy.15
  223.7 0.7 copy-done.1
  224.4 0.0 copy-start
  224.4 1.0 copy.16
  225.4 0.7 copy-done
  226.1 1.0 copy.17
Async XLA Ops:
  220.3 2.5 %copy-start.2 = (bf16[384,1536]{1,0:T(8,128)(2,1)S(1)}, bf16[384,1536]{1,0:T(8,128)(2,1)}, u32[]{:S(2)}) copy-start(bf16[384,1536]{1,0:T(8,128)(2,1)} %get-tuple-element.9) | copy-start | bytes 3538948
  222.7 1.7 copy-start.1
  224.4 1.7 copy-start

commit v5 on v4

--- a/solution.py
+++ b/solution.py
@@ -10,8 +10,7 @@
 
 HS = 128
 GROUPS = 6
-DEPTH = 2
-AHEAD = 4
+DEPTH = 3
 MESH = pl.DeviceIdType.MESH
 LOG2E = math.log2(math.e)
 HIDDEN = -1e30
@@ -181,39 +180,31 @@
         def _():
             kv_copy(a, 0, g, kv_src[a], s).wait_recv()
 
-    def stream(i, f):
-        for a in range(2):
-            pl.when((i >= a * GROUPS) & (i < (a + 1) * GROUPS))(lambda: f(a, i - a * GROUPS))
-
-    def qo_start(i):
-        def start(a, g):
-            in_turn(
-                (odd, lambda: qo_copy(a, 0, g, qo_src[a], s - 1).start()),
-                (s >= 2, lambda: qo_copy(a, 1, g, qo_src[a], s - 2).start()),
-            )
-
-        stream(i, start)
-
-    def qo_pass(k):
-        passes = even & (s + 2 < n)
-
+    half = GROUPS // 2
+
+    def qo_start(a, g):
+        in_turn(
+            (odd, lambda: qo_copy(a, 0, g, qo_src[a], s - 1).start()),
+            (s >= 2, lambda: qo_copy(a, 1, g, qo_src[a], s - 2).start()),
+        )
+
+    def qo_left(a, g):
+        @pl.when(odd)
+        def _():
+            qo_copy(a, 0, g, qo_src[a], s).wait_send()
+
+        @pl.when(s >= 2)
+        def _():
+            qo_copy(a, 1, g, qo_src[a], s).wait_send()
+
+    def qo_pass(a, g):
         @pl.when(s + 2 < n)
         def _():
-            stream(k, lambda a, g: qo_copy(a, 1, g, qo_src[a], s).wait_recv())
-
-        pl.when(passes)(
-            lambda: stream(k, lambda a, g: qo_copy(a, 0, g, qo_buf.at[a, 1], s + 1).start())
-        )
-
-        @pl.when(odd)
-        def _():
-            stream(k, lambda a, g: qo_copy(a, 0, g, qo_src[a], s).wait_send())
-
-        @pl.when(s >= 2)
-        def _():
-            stream(k, lambda a, g: qo_copy(a, 1, g, qo_src[a], s).wait_send())
-
-        qo_start(k + AHEAD)
+            qo_copy(a, 1, g, qo_src[a], s).wait_recv()
+
+            @pl.when(even)
+            def _():
+                qo_copy(a, 0, g, qo_buf.at[a, 1], s + 1).start()
 
     def qo_near_arrive(g):
         @pl.when(s + 1 < n)
@@ -300,21 +291,24 @@
         sums[1] += cot_ref[:, c].astype(jnp.float32) * gain_ref[:, c] * att
 
     def forward_group(g):
-        for a in range(2):
-            kv_pass(a, g)
-        for a in range(2):
-            kv_next(a, g)
-        for a in range(2):
-            kv_near_arrive(a, g)
+        @pl.when(g < GROUPS)
+        def _():
+            for a in range(2):
+                kv_pass(a, g)
+            for a in range(2):
+                kv_next(a, g)
 
         @pl.when(g == GROUPS - 1)
         def _():
-            for k in range(AHEAD):
-                qo_start(k)
-
-        loop(per_group, lambda i: forward_head(g * per_group + i))
-
-    loop(GROUPS, forward_group)
+            loop(GROUPS, lambda i: qo_start(0, i))
+
+        @pl.when(g >= 1)
+        def _():
+            for a in range(2):
+                kv_near_arrive(a, g - 1)
+            loop(per_group, lambda i: forward_head((g - 1) * per_group + i))
+
+    loop(GROUPS + 1, forward_group)
 
     def sums_copy(j):
         return pltpu.make_async_remote_copy(
@@ -351,6 +345,7 @@
 
     def norm_group(g):
         loop(per_group, lambda i: norm_head(g * per_group + i))
+        pl.when(g < half)(lambda: qo_start(1, g))
 
     loop(GROUPS, norm_group)
     for i in range(2):
@@ -401,17 +396,21 @@
         dk_ref[:, c] = ((dk_acc[:, c] + dk) * scale).astype(dk_ref.dtype)
         dv_ref[:, c] = (dv_acc[:, c] + dv).astype(dv_ref.dtype)
 
-    for k in range(2):
-        qo_pass(k)
+    def second_half(i):
+        qo_left(1, i)
+        qo_start(1, i + half)
 
     def local_group(g):
-        for i in range(per_group):
-            local_head(g * per_group + i)
-            if i < 2:
-                qo_pass(2 * g + 2 + i)
-
-    half = GROUPS // 2
-    loop(half, local_group)
+        loop(per_group, lambda i: local_head(g * per_group + i))
+        pl.when(g == 1)(lambda: loop(half, lambda i: qo_pass(0, i)))
+        pl.when(g == 2)(lambda: loop(half, lambda i: qo_pass(0, half + i)))
+
+        @pl.when(g == GROUPS - 2)
+        def _():
+            loop(half, second_half)
+            loop(half, lambda i: qo_pass(1, i))
+
+    loop(GROUPS, local_group)
 
     for slot in range(2):
         @pl.when(s + slot + 1 < n)
@@ -421,14 +420,11 @@
             ).wait_recv()
 
     def remote_group(g):
+        pl.when(g == 1)(lambda: loop(half, lambda i: qo_pass(1, half + i)))
         qo_near_arrive(g)
         loop(per_group, lambda i: remote_head(g * per_group + i))
 
-    def both_groups(i):
-        local_group(half + i)
-        loop(2, lambda j: remote_group(2 * i + j))
-
-    loop(half, both_groups)
+    loop(GROUPS, remote_group)
 
     for slot in range(2):
         @pl.when(s >= slot + 1)
@@ -444,6 +440,9 @@
             @pl.when(even & (s + 2 < n))
             def _():
                 qo_copy(a, 0, g, qo_src[a], s).wait_send()
+
+        qo_left(0, g)
+        pl.when(g >= half)(lambda: qo_left(1, g))
 
     loop(GROUPS, sent)
 

time: 227 us -> 218 us (0.960)
  the two profiles are of different devices: /device:TPU:14 before, /device:TPU:22 now
where the time goes in v5:
time: 218 us
  Pallas kernels  208 us (95%)
  local copies, waits for them, and re-layouts  9.4 us (4%)
    pallas_call x1, Pallas kernels, body(): pl.pallas_call(functools.partial(kernel, n, tp), out_shape=(out,) * 4, in...  208 us
    unnamed x10, local copies, waits for them, and re-layouts  6.86 us

profile of v5, /device:TPU:22, one launch (start us, length us, event | category | flops | bytes accessed | tf_op | source)
XLA Modules:
  0.0 217.7 jit_solution(5514952547904161071)
XLA Ops:
  0.6 1.2 reshape.14.doc_ref
  1.9 1.3 reshape.15.gain_ref
  3.2 207.6 %shard_map.93 = (bf16[384,1536]{1,0:T(8,128)(2,1)}, bf16[384,1536]{1,0:T(8,128)(2,1)}, bf16[384,1536]{1,0:T(8,128)(2,1)}, bf16[384,1536]{1,0:T(8,128)(2,1)}) custom-call(bf16[384,1536]{1,0:T(8,128)(2,1)} %q_ref.1, bf16[384,1536]{1,0:T(8,128)(2,1)} %k_ref.1, bf16[384,1536]{1,0:T(8,128)(2,1)} %v_ref.1, bf16[384,1536]{1,0:T(8,128)(2,1)} %cot_ref.1, ...), custom_call_target="tpu_custom_call" | custom-call | flops 10871635968 | bytes 9437184 | tf_op jit(solution)/shard_map/pallas_call | solution.py:458
  210.8 0.0 copy-start.2
  210.8 2.5 %copy.14 = bf16[384,1536]{1,0:T(8,128)(2,1)} copy(bf16[384,1536]{1,0:T(8,128)(2,1)} %get-tuple-element.8) | data formatting | bytes 2359296
  213.3 0.0 copy-done.2
  213.3 0.0 copy-start.1
  213.3 1.0 copy.15
  214.3 0.7 copy-done.1
  215.0 0.0 copy-start
  215.0 1.0 copy.16
  216.0 0.7 copy-done
  216.7 1.0 copy.17
Async XLA Ops:
  210.8 2.5 %copy-start.2 = (bf16[384,1536]{1,0:T(8,128)(2,1)S(1)}, bf16[384,1536]{1,0:T(8,128)(2,1)}, u32[]{:S(2)}) copy-start(bf16[384,1536]{1,0:T(8,128)(2,1)} %get-tuple-element.9) | copy-start | bytes 3538948
  213.3 1.7 copy-start.1
  215.0 1.7 copy-start

commit v6 on v2

--- a/solution.py
+++ b/solution.py
@@ -10,6 +10,7 @@
 
 HS = 128
 GROUPS = 6
+PASSED = 3
 MESH = pl.DeviceIdType.MESH
 LOG2E = math.log2(math.e)
 HIDDEN = -1e30
@@ -140,7 +141,7 @@
 
     def kv_start(g):
         for a in range(2):
-            @pl.when(even)
+            @pl.when(even | ((g >= PASSED) & (s + 2 < n)))
             def _():
                 kv_copy(a, 0, g, kv_src[a], s + 1).start()
 
@@ -149,7 +150,7 @@
                 kv_copy(a, 1, g, kv_src[a], s + 2).start()
 
     def qo_start(a, g):
-        @pl.when(odd)
+        @pl.when(odd | ((g >= PASSED) & (s >= 2)))
         def _():
             qo_copy(a, 0, g, qo_src[a], s - 1).start()
 
@@ -163,7 +164,7 @@
             for a in range(2):
                 kv_copy(a, 1, g, kv_src[a], s).wait_recv()
 
-                @pl.when(odd)
+                @pl.when(odd & (g < PASSED))
                 def _():
                     kv_copy(a, 0, g, kv_buf.at[a, 1], s - 1).start()
 
@@ -177,7 +178,7 @@
         def _():
             qo_copy(a, 1, g, qo_src[a], s).wait_recv()
 
-            @pl.when(even)
+            @pl.when(even & (g < PASSED))
             def _():
                 qo_copy(a, 0, g, qo_buf.at[a, 1], s + 1).start()
 
@@ -391,7 +392,7 @@
 
     def sent(g):
         for a in range(2):
-            @pl.when(even | (s >= 3))
+            @pl.when(even | ((g < PASSED) & (s >= 3)) | ((g >= PASSED) & (s + 2 < n)))
             def _():
                 kv_copy(a, 0, g, kv_src[a], s).wait_send()
 
@@ -399,7 +400,7 @@
             def _():
                 kv_copy(a, 1, g, kv_src[a], s).wait_send()
 
-            @pl.when(odd | (s + 3 < n))
+            @pl.when(odd | ((g < PASSED) & (s + 3 < n)) | ((g >= PASSED) & (s >= 2)))
             def _():
                 qo_copy(a, 0, g, qo_src[a], s).wait_send()
 

time: 189 us -> 202 us (1.069)
  Pallas kernels: 178 us -> 191 us
    pallas_call x1, Pallas kernels: 178 us -> 191 us  [body(): pl.pallas_call(functools.partial(kernel, n, tp), out_shape=(out,) * 4, in...]
where the time goes in v6:
time: 202 us; the launch traced here: 201 us
  Pallas kernels  191 us (95%)
  local copies, waits for them, and re-layouts  9.4 us (5%)
    pallas_call x1, Pallas kernels, body(): pl.pallas_call(functools.partial(kernel, n, tp), out_shape=(out,) * 4, in...  191 us
    unnamed x10, local copies, waits for them, and re-layouts  6.86 us

profile of v6, /device:TPU:14, one launch (start us, length us, event | category | flops | bytes accessed | tf_op | source)
XLA Modules:
  0.0 201.3 jit_solution(5509301136495820695)
XLA Ops:
  0.6 1.2 reshape.14.doc_ref
  1.9 1.3 reshape.15.gain_ref
  3.2 191.3 %shard_map.93 = (bf16[384,1536]{1,0:T(8,128)(2,1)}, bf16[384,1536]{1,0:T(8,128)(2,1)}, bf16[384,1536]{1,0:T(8,128)(2,1)}, bf16[384,1536]{1,0:T(8,128)(2,1)}) custom-call(bf16[384,1536]{1,0:T(8,128)(2,1)} %q_ref.1, bf16[384,1536]{1,0:T(8,128)(2,1)} %k_ref.1, bf16[384,1536]{1,0:T(8,128)(2,1)} %v_ref.1, bf16[384,1536]{1,0:T(8,128)(2,1)} %cot_ref.1, ...), custom_call_target="tpu_custom_call" | custom-call | flops 10871635968 | bytes 9437184 | tf_op jit(solution)/shard_map/pallas_call | solution.py:422
  194.4 0.0 copy-start.2
  194.4 2.5 %copy.14 = bf16[384,1536]{1,0:T(8,128)(2,1)} copy(bf16[384,1536]{1,0:T(8,128)(2,1)} %get-tuple-element.8) | data formatting | bytes 2359296
  196.9 0.0 copy-done.2
  196.9 0.0 copy-start.1
  196.9 1.0 copy.15
  197.9 0.7 copy-done.1
  198.6 0.0 copy-start
  198.6 1.0 copy.16
  199.6 0.7 copy-done
  200.3 1.0 copy.17
Async XLA Ops:
  194.4 2.5 %copy-start.2 = (bf16[384,1536]{1,0:T(8,128)(2,1)S(1)}, bf16[384,1536]{1,0:T(8,128)(2,1)}, u32[]{:S(2)}) copy-start(bf16[384,1536]{1,0:T(8,128)(2,1)} %get-tuple-element.9) | copy-start | bytes 3538948
  196.9 1.7 copy-start.1
  198.6 1.7 copy-start

commit v7 on v2

--- a/solution.py
+++ b/solution.py
@@ -157,15 +157,18 @@
         def _():
             qo_copy(a, 1, g, qo_src[a], s - 2).start()
 
-    def kv_arrive(g):
+    def kv_pass(g):
         @pl.when(s >= 2)
         def _():
             for a in range(2):
                 kv_copy(a, 1, g, kv_src[a], s).wait_recv()
-
-                @pl.when(odd)
-                def _():
-                    kv_copy(a, 0, g, kv_buf.at[a, 1], s - 1).start()
+                kv_copy(a, 0, g, kv_buf.at[a, 1], s - 1).start()
+
+    def kv_arrive(g):
+        @pl.when(even & (s >= 2))
+        def _():
+            for a in range(2):
+                kv_copy(a, 1, g, kv_src[a], s).wait_recv()
 
         @pl.when(s >= 1)
         def _():
@@ -190,7 +193,9 @@
     def loop(count, f):
         lax.fori_loop(0, count, lambda i, c: (f(i), c)[1], 0)
 
-    loop(GROUPS, kv_start)
+    half = GROUPS // 2
+    loop(half, kv_start)
+    pl.when(even)(lambda: loop(half, lambda i: kv_start(half + i)))
 
     for slot in range(2):
         @pl.when(s < slot + 1)
@@ -271,6 +276,12 @@
             loop(GROUPS, lambda i: qo_start(0, i))
 
         loop(per_group, lambda i: forward_head(g * per_group + i))
+
+    @pl.when(odd)
+    def _():
+        loop(half, kv_pass)
+        loop(half, lambda i: kv_start(half + i))
+        loop(half, lambda i: kv_pass(half + i))
 
     loop(GROUPS, forward_group)
 

time: 189 us -> 163 us (0.86)
  Pallas kernels: 178 us -> 152 us
    pallas_call x1, Pallas kernels: 178 us -> 152 us  [body(): pl.pallas_call(functools.partial(kernel, n, tp), out_shape=(out,) * 4, in...]
where the time goes in v7:
time: 163 us
  Pallas kernels  152 us (93%)
  local copies, waits for them, and re-layouts  9.4 us (6%)
    pallas_call x1, Pallas kernels, body(): pl.pallas_call(functools.partial(kernel, n, tp), out_shape=(out,) * 4, in...  152 us
    unnamed x10, local copies, waits for them, and re-layouts  6.86 us

profile of v7, /device:TPU:14, one launch (start us, length us, event | category | flops | bytes accessed | tf_op | source)
XLA Modules:
  0.0 162.5 jit_solution(5976361898715967909)
XLA Ops:
  0.6 1.2 reshape.14.doc_ref
  1.9 1.3 reshape.15.gain_ref
  3.2 152.5 %shard_map.93 = (bf16[384,1536]{1,0:T(8,128)(2,1)}, bf16[384,1536]{1,0:T(8,128)(2,1)}, bf16[384,1536]{1,0:T(8,128)(2,1)}, bf16[384,1536]{1,0:T(8,128)(2,1)}) custom-call(bf16[384,1536]{1,0:T(8,128)(2,1)} %q_ref.1, bf16[384,1536]{1,0:T(8,128)(2,1)} %k_ref.1, bf16[384,1536]{1,0:T(8,128)(2,1)} %v_ref.1, bf16[384,1536]{1,0:T(8,128)(2,1)} %cot_ref.1, ...), custom_call_target="tpu_custom_call" | custom-call | flops 10871635968 | bytes 9437184 | tf_op jit(solution)/shard_map/pallas_call | solution.py:432
  155.7 0.0 copy-start.2
  155.7 2.5 %copy.14 = bf16[384,1536]{1,0:T(8,128)(2,1)} copy(bf16[384,1536]{1,0:T(8,128)(2,1)} %get-tuple-element.8) | data formatting | bytes 2359296
  158.1 0.0 copy-done.2
  158.1 0.0 copy-start.1
  158.1 1.0 copy.15
  159.2 0.7 copy-done.1
  159.8 0.0 copy-start
  159.8 1.0 copy.16
  160.9 0.7 copy-done
  161.5 1.0 copy.17
Async XLA Ops:
  155.7 2.5 %copy-start.2 = (bf16[384,1536]{1,0:T(8,128)(2,1)S(1)}, bf16[384,1536]{1,0:T(8,128)(2,1)}, u32[]{:S(2)}) copy-start(bf16[384,1536]{1,0:T(8,128)(2,1)} %get-tuple-element.9) | copy-start | bytes 3538948
  158.1 1.7 %copy-start.1 = (bf16[384,1536]{1,0:T(8,128)(2,1)S(1)}, bf16[384,1536]{1,0:T(8,128)(2,1)}, u32[]{:S(2)}) copy-start(bf16[384,1536]{1,0:T(8,128)(2,1)} %get-tuple-element.10) | copy-start | bytes 3538948
  159.8 1.7 %copy-start = (bf16[384,1536]{1,0:T(8,128)(2,1)S(1)}, bf16[384,1536]{1,0:T(8,128)(2,1)}, u32[]{:S(2)}) copy-start(bf16[384,1536]{1,0:T(8,128)(2,1)} %get-tuple-element.11) | copy-start | bytes 3538948
